TPU v7x, 32 devices: a whole 2x2x4 slice. The times are simulated.
32 devices in a mesh: groups: 2 (over y), outer: 4 (over z), inner: 2 (over x), heads: 2 (over core).
Axes of the slice: x: 2, y: 2, z: 4, core: 2. Of those that a mesh axis runs over, the one named last changes fastest.
Arguments:
- queries: bfloat16 [2048, 8192], P(('groups', 'outer', 'inner'), 'heads'), parts along dimension 0, may hold values from -4.5 to 4.5
- keys: bfloat16 [2048, 1024], P(('groups', 'outer', 'inner'), 'heads'), parts along dimension 0, may hold values from -4.5 to 4.5
- values: bfloat16 [2048, 1024], P(('groups', 'outer', 'inner'), 'heads'), parts along dimension 0, may hold values from -4.5 to 4.5
- prefix_keys: bfloat16 [128, 1024], P('groups', 'heads'), parts along dimension 0, may hold values from -5 to 5
- prefix_values: bfloat16 [128, 1024], P('groups', 'heads'), parts along dimension 0, may hold values from -4.5 to 4.5
Outputs:
- attended: bfloat16 [2048, 8192], P(('groups', 'outer', 'inner'), 'heads'), parts along dimension 0
There are 2 independent parts, one for each index of `groups`. A program takes and returns all parts, laid end to end along the dimension named above; each array names one. Nothing has to cross between parts.
All inputs are finite; a program needn't handle non-finite values.
Results may differ from a plain program's by a relative error of at most 0.006.
Values may be sent and summed in bfloat16 or wider, within the bound.
A program may use at most 64 MiB of HBM per device.

v0:
```python
import jax
import jax.numpy as jnp
from jax import lax
from jax.sharding import PartitionSpec as P

HD = 128
GQ = 8
WINDOW = 256


def passed_along(value, axis, steps):
    count = lax.axis_size(axis)
    leading, last = (max(0, -steps), min(count, count - steps))
    return lax.ppermute(value, axis, [(source, source + steps) for source in range(leading, last)])


def slot_positions(slot_number, slot_count, block_rows):
    last_block = 2 * slot_count - 1 - slot_number
    offsets = jnp.arange(2 * block_rows, dtype=jnp.int32)
    return jnp.where(
        offsets < block_rows,
        slot_number * block_rows + offsets,
        last_block * block_rows + offsets - block_rows,
    )


def opening(query_part, pre_keys, pre_values):
    scores = jnp.einsum(
        "rkgd,nkd->kgrn", query_part, pre_keys, preferred_element_type=jnp.float32
    ) * (1.0 / HD**0.5)
    top_score = jnp.max(scores, axis=-1)
    exps = jnp.exp(scores - top_score[..., None])
    summed = jnp.einsum(
        "kgrn,nkd->kgrd", exps.astype(jnp.bfloat16), pre_values, preferred_element_type=jnp.float32
    )
    return (top_score, jnp.sum(exps, axis=-1), summed)


def absorb(carry_state, query_part, key_tile, value_tile, visible):
    top_score, total, summed = carry_state
    scores = jnp.einsum(
        "rkgd,nkd->kgrn", query_part, key_tile, preferred_element_type=jnp.float32
    ) * (1.0 / HD**0.5)
    scores = jnp.where(visible[None, None], scores, -jnp.inf)
    new_top = jnp.maximum(top_score, jnp.max(scores, axis=-1))
    factor = jnp.exp(top_score - new_top)
    exps = jnp.exp(scores - new_top[..., None])
    total = total * factor + jnp.sum(exps, axis=-1)
    summed = summed * factor[..., None] + jnp.einsum(
        "kgrn,nkd->kgrd", exps.astype(jnp.bfloat16), value_tile, preferred_element_type=jnp.float32
    )
    return (new_top, total, summed)


def local(queries, keys, values, prefix_keys, prefix_values):
    row_count = queries.shape[0]
    block_rows = row_count // 2
    kv_heads = keys.shape[1] // HD
    reach = WINDOW // block_rows
    grid_q = queries.reshape(row_count, kv_heads, GQ, HD)
    slot_index = lax.axis_index(("outer", "inner"))
    slot_count = lax.axis_size(("outer", "inner"))
    query_positions = slot_positions(slot_index, slot_count, block_rows)
    halves = [grid_q[:block_rows], grid_q[block_rows:]]
    pre_keys = prefix_keys.reshape(-1, kv_heads, HD)
    pre_values = prefix_values.reshape(-1, kv_heads, HD)
    carry_states = [opening(half_rows, pre_keys, pre_values) for half_rows in halves]

    def visit_block(old_states, block_keys, block_values, source):
        present = (source >= 0) & (source < slot_count)
        key_positions = slot_positions(source, slot_count, block_rows)
        key_grid = block_keys.reshape(row_count, kv_heads, HD)
        value_grid = block_values.reshape(row_count, kv_heads, HD)
        new_states = []
        for half_index in range(2):
            lower = half_index * block_rows
            half_positions = query_positions[lower : lower + block_rows]
            visible = (
                present
                & (key_positions[None, :] <= half_positions[:, None])
                & (key_positions[None, :] > half_positions[:, None] - WINDOW)
            )
            new_states.append(
                absorb(old_states[half_index], halves[half_index], key_grid, value_grid, visible)
            )
        return new_states

    carry_states = visit_block(carry_states, keys, values, slot_index)
    upward = (keys, values)
    downward = (keys, values)
    for distance in range(1, reach + 1):
        upward = passed_along((upward[0], upward[1]), ("outer", "inner"), 1)
        downward = passed_along((downward[0], downward[1]), ("outer", "inner"), -1)
        carry_states = visit_block(carry_states, upward[0], upward[1], slot_index - distance)
        carry_states = visit_block(carry_states, downward[0], downward[1], slot_index + distance)
    pieces = [carry_state[2] / carry_state[1][..., None] for carry_state in carry_states]
    joined = jnp.concatenate(pieces, axis=2)
    return joined.transpose(2, 0, 1, 3).reshape(row_count, kv_heads * GQ * HD).astype(jnp.bfloat16)


def solution(mesh):
    placed = (
        P(("groups", "outer", "inner"), "heads"),
        P(("groups", "outer", "inner"), "heads"),
        P(("groups", "outer", "inner"), "heads"),
        P("groups", "heads"),
        P("groups", "heads"),
    )
    return jax.shard_map(
        local,
        mesh=mesh,
        in_specs=placed,
        out_specs=P(("groups", "outer", "inner"), "heads"),
        check_vma=False,
    )
```

profile of v0, /device:TPU:0, one launch (start us, length us, event | category | flops | bytes accessed | tf_op | source)
XLA Modules:
  0.0 117.9 jit_solution(8431377850270246007)
XLA Ops:
  0.0 1.7 %copy.23 = bf16[128,512]{0,1:T(8,128)(2,1)} copy(bf16[128,512]{1,0:T(8,128)(2,1)} %param.6) | data formatting | bytes 262144 | tf_op args[1]
  1.7 5.5 %collective-permute-start = (bf16[128,512]{0,1:T(8,128)(2,1)}, bf16[128,512]{0,1:T(8,128)(2,1)}, u32[]{:S(2)}, u32[]{:S(2)}) collective-permute-start(bf16[128,512]{0,1:T(8,128)(2,1)} %copy.23), channel_id=1, source_target_pairs={{0,2},{2,4},{4,6},{6,8},{8,10},{10,12},{12,14},{1,3},{3,5},{5,7},{... | collective-permute-start | bytes 393224 | tf_op jit(solution)/shard_map/ppermute | solution.py:14
  7.2 1.3 %collective-permute-start.2 = (bf16[128,512]{0,1:T(8,128)(2,1)}, bf16[128,512]{0,1:T(8,128)(2,1)}, u32[]{:S(2)}, u32[]{:S(2)}) collective-permute-start(bf16[128,512]{0,1:T(8,128)(2,1)} %copy.23), channel_id=1, source_target_pairs={{2,0},{4,2},{6,4},{8,6},{10,8},{12,10},{14,12},{3,1},{5,3},{7,5},{... | collective-permute-start | bytes 393224 | tf_op jit(solution)/shard_map/ppermute | solution.py:14
  8.5 1.7 %copy.26 = bf16[128,512]{0,1:T(8,128)(2,1)} copy(bf16[128,512]{1,0:T(8,128)(2,1)} %param.7) | data formatting | bytes 262144 | tf_op args[2]
  10.2 1.3 %collective-permute-start.3 = (bf16[128,512]{0,1:T(8,128)(2,1)}, bf16[128,512]{0,1:T(8,128)(2,1)}, u32[]{:S(2)}, u32[]{:S(2)}) collective-permute-start(bf16[128,512]{0,1:T(8,128)(2,1)} %copy.26), channel_id=1, source_target_pairs={{2,0},{4,2},{6,4},{8,6},{10,8},{12,10},{14,12},{3,1},{5,3},{7,5},{... | collective-permute-start | bytes 393224 | tf_op jit(solution)/shard_map/ppermute | solution.py:14
  11.5 5.2 %collective-permute-start.1 = (bf16[128,512]{0,1:T(8,128)(2,1)}, bf16[128,512]{0,1:T(8,128)(2,1)S(1)}, u32[]{:S(2)}, u32[]{:S(2)}) collective-permute-start(bf16[128,512]{0,1:T(8,128)(2,1)} %copy.26), channel_id=1, source_target_pairs={{0,2},{2,4},{4,6},{6,8},{8,10},{10,12},{12,14},{1,3},{3,5},{5,7},{... | collective-permute-start | bytes 393224 | tf_op jit(solution)/shard_map/ppermute | solution.py:14
  16.7 1.6 %reshape.1671 = bf16[128,4,128]{2,1,0:T(4,128)(2,1)} reshape(bf16[128,512]{1,0:T(8,128)(2,1)} %param.6) | data formatting | bytes 262144 | tf_op jit(solution)/shard_map/reshape | solution.py:72
  18.3 0.9 reshape.1672
  19.9 0.7 fusion.184
  20.7 0.7 copy-done.5
  21.6 1.2 %fusion.203 = (f32[4,8,64]{2,1,0:T(8,128)}, f32[4,8,64,64]{2,3,1,0:T(8,128)S(1)}) fusion(bf16[64,4,8,128]{3,2,1,0:T(8,128)(2,1)S(1)} %bitcast.233, bf16[64,4,128,1]{2,1,0,3:T(4,128)(2,1)S(1)} %bitcast.248), kind=kOutput, calls=%fused_computation.288 | convolution fusion | flops 33814528 | bytes 1122304 | tf_op jit(solution)/shard_map/rkgd,nkd->kgrn/dot_general | solution.py:28
  23.6 1.5 %compare_and_fusion.17 = (pred[64,128]{1,0:T(8,128)(4,1)S(1)}, pred[64,128]{1,0:T(8,128)(4,1)}, pred[64,128]{1,0:T(8,128)(4,1)}, pred[64,128]{1,0:T(8,128)(4,1)}...) fusion(s32[128]{0:T(128)} %copy-done.19, ...), kind=kLoop, calls=%fused_computation.214 | loop fusion | flops 262144 | bytes 70152 | tf_op jit(solution)/shard_map/and | solution.py:79
  25.1 2.9 %fusion.204 = (f32[4,8,64]{2,1,0:T(8,128)}, f32[4,8,64,128]{3,2,1,0:T(8,128)}) fusion(bf16[64,4,8,128]{3,2,1,0:T(8,128)(2,1)S(1)} %bitcast.234, bf16[128,4,128,1]{2,1,0,3:T(4,128)(2,1)} %bitcast.274, pred[64,128]{1,0:T(8,128)(4,1)S(1)} %get-tuple-element.45), kind=kOutput, calls=%fused_computation.289 | convolution fusion | flops 67893248 | bytes 1720320 | tf_op jit(solution)/shard_map/rkgd,nkd->kgrn/dot_general | solution.py:41
  28.0 1.4 %compare_and_fusion.8 = (pred[64,128]{1,0:T(8,128)(4,1)S(1)}, pred[64,128]{1,0:T(8,128)(4,1)}, pred[64,128]{1,0:T(8,128)(4,1)}, pred[64,128]{1,0:T(8,128)(4,1)},...) fusion(s32[128]{0:T(128)S(1)} %copy-done.20, ...), kind=kLoop, calls=%fused_computation.205 | loop fusion | flops 262144 | bytes 70152 | tf_op jit(solution)/shard_map/and | solution.py:79
  29.4 2.0 %fusion.194 = (f32[4,8,64]{2,1,0:T(8,128)}, f32[4,8,64,128]{3,2,1,0:T(8,128)}) fusion(bf16[64,4,8,128]{3,2,1,0:T(8,128)(2,1)S(1)} %bitcast.224, bf16[128,4,128,1]{2,1,0,3:T(4,128)(2,1)S(1)} %bitcast.275, pred[64,128]{1,0:T(8,128)(4,1)S(1)} %get-tuple-element.53), kind=kOutput, calls=%fused_computation.279 | convolution fusion | flops 67893248 | bytes 1720320 | tf_op jit(solution)/shard_map/rkgd,nkd->kgrn/dot_general | solution.py:41
  31.4 0.8 compare_and_fusion.9
  32.9 1.4 %fusion.201 = (f32[4,8,64]{2,1,0:T(8,128)S(1)}, f32[4,8,64,128]{3,2,1,0:T(8,128)S(1)}) fusion(bf16[128,4,128,1]{0,2,3,1:T(8,128)(2,1)} %bitcast.83, bf16[64,4,8,128]{3,2,1,0:T(8,128)(2,1)S(1)} %bitcast.235, pred[64,128]{1,0:T(8,128)(4,1)S(1)} %copy-done.15), kind=kOutput, calls=%fused_computation.286 | convolution fusion | flops 67893248 | bytes 1720320 | tf_op jit(solution)/shard_map/rkgd,nkd->kgrn/dot_general | solution.py:41
  34.3 1.4 %fusion.191 = (f32[4,8,64]{2,1,0:T(8,128)S(1)}, f32[4,8,64,128]{3,2,1,0:T(8,128)S(1)}) fusion(bf16[128,4,128,1]{0,2,3,1:T(8,128)(2,1)} %bitcast.83, bf16[64,4,8,128]{3,2,1,0:T(8,128)(2,1)S(1)} %bitcast.225, pred[64,128]{1,0:T(8,128)(4,1)S(1)} %copy-done.16), kind=kOutput, calls=%fused_computation.276 | convolution fusion | flops 67893248 | bytes 1720320 | tf_op jit(solution)/shard_map/rkgd,nkd->kgrn/dot_general | solution.py:41
  35.8 1.4 %fusion.202 = (f32[4,8,64]{2,1,0:T(8,128)S(1)}, f32[4,8,64,128]{3,2,1,0:T(8,128)S(1)}) fusion(bf16[128,4,128,1]{0,2,3,1:T(8,128)(2,1)} %bitcast.79, bf16[64,4,8,128]{3,2,1,0:T(8,128)(2,1)S(1)} %bitcast.236, pred[64,128]{1,0:T(8,128)(4,1)S(1)} %copy-done.13), kind=kOutput, calls=%fused_computation.287 | convolution fusion | flops 67893248 | bytes 1720320 | tf_op jit(solution)/shard_map/rkgd,nkd->kgrn/dot_general | solution.py:41
  37.2 1.3 %collective-permute-start.6 = (bf16[128,512]{0,1:T(8,128)(2,1)}, bf16[128,512]{0,1:T(8,128)(2,1)S(1)}, u32[]{:S(2)}, u32[]{:S(2)}) collective-permute-start(bf16[128,512]{0,1:T(8,128)(2,1)} %collective-permute-done.2), channel_id=1, source_target_pairs={{2,0},{4,2},{6,4},{8,6},{10,8},{12,10},{14,12},{3,1},{5,3},{7,5},{... | collective-permute-start | bytes 393224 | tf_op jit(solution)/shard_map/ppermute | solution.py:14
  38.5 1.4 %fusion.192 = (f32[4,8,64]{2,1,0:T(8,128)S(1)}, f32[4,8,64,128]{3,2,1,0:T(8,128)S(1)}) fusion(bf16[128,4,128,1]{0,2,3,1:T(8,128)(2,1)} %bitcast.79, bf16[64,4,8,128]{3,2,1,0:T(8,128)(2,1)S(1)} %bitcast.226, pred[64,128]{1,0:T(8,128)(4,1)S(1)} %copy-done.14), kind=kOutput, calls=%fused_computation.277 | convolution fusion | flops 67893248 | bytes 1720320 | tf_op jit(solution)/shard_map/rkgd,nkd->kgrn/dot_general | solution.py:41
  40.0 5.5 %collective-permute-start.4 = (bf16[128,512]{0,1:T(8,128)(2,1)}, bf16[128,512]{0,1:T(8,128)(2,1)S(1)}, u32[]{:S(2)}, u32[]{:S(2)}) collective-permute-start(bf16[128,512]{0,1:T(8,128)(2,1)} %collective-permute-done), channel_id=1, source_target_pairs={{0,2},{2,4},{4,6},{6,8},{8,10},{10,12},{12,14},{1,3},{3,5},{5,7},{... | collective-permute-start | bytes 393224 | tf_op jit(solution)/shard_map/ppermute | solution.py:14
  45.4 1.3 %collective-permute-start.7 = (bf16[128,512]{0,1:T(8,128)(2,1)}, bf16[128,512]{0,1:T(8,128)(2,1)S(1)}, u32[]{:S(2)}, u32[]{:S(2)}) collective-permute-start(bf16[128,512]{0,1:T(8,128)(2,1)} %collective-permute-done.3), channel_id=1, source_target_pairs={{2,0},{4,2},{6,4},{8,6},{10,8},{12,10},{14,12},{3,1},{5,3},{7,5},{... | collective-permute-start | bytes 393224 | tf_op jit(solution)/shard_map/ppermute | solution.py:14
  46.7 5.4 %collective-permute-start.5 = (bf16[128,512]{0,1:T(8,128)(2,1)S(1)}, bf16[128,512]{0,1:T(8,128)(2,1)S(1)}, u32[]{:S(2)}, u32[]{:S(2)}) collective-permute-start(bf16[128,512]{0,1:T(8,128)(2,1)S(1)} %collective-permute-done.1), channel_id=1, source_target_pairs={{0,2},{2,4},{4,6},{6,8},{8,10},{10,12},{12,14},{1,3},{3,5},{5,7},{... | collective-permute-start | bytes 393224 | tf_op jit(solution)/shard_map/ppermute | solution.py:14
  53.9 1.3 %collective-permute-start.10 = (bf16[128,512]{0,1:T(8,128)(2,1)S(1)}, bf16[128,512]{0,1:T(8,128)(2,1)S(1)}, u32[]{:S(2)}, u32[]{:S(2)}) collective-permute-start(bf16[128,512]{0,1:T(8,128)(2,1)S(1)} %collective-permute-done.6), channel_id=1, source_target_pairs={{2,0},{4,2},{6,4},{8,6},{10,8},{12,10},{14,12},{3,1},{5,3},{7,5},{... | collective-permute-start | bytes 393224 | tf_op jit(solution)/shard_map/ppermute | solution.py:14
  55.8 5.5 %collective-permute-start.8 = (bf16[128,512]{0,1:T(8,128)(2,1)S(1)}, bf16[128,512]{0,1:T(8,128)(2,1)S(1)}, u32[]{:S(2)}, u32[]{:S(2)}) collective-permute-start(bf16[128,512]{0,1:T(8,128)(2,1)S(1)} %collective-permute-done.4), channel_id=1, source_target_pairs={{0,2},{2,4},{4,6},{6,8},{8,10},{10,12},{12,14},{1,3},{3,5},{5,7},{... | collective-permute-start | bytes 393224 | tf_op jit(solution)/shard_map/ppermute | solution.py:14
  61.2 1.3 %collective-permute-start.11 = (bf16[128,512]{0,1:T(8,128)(2,1)S(1)}, bf16[128,512]{0,1:T(8,128)(2,1)S(1)}, u32[]{:S(2)}, u32[]{:S(2)}) collective-permute-start(bf16[128,512]{0,1:T(8,128)(2,1)S(1)} %collective-permute-done.7), channel_id=1, source_target_pairs={{2,0},{4,2},{6,4},{8,6},{10,8},{12,10},{14,12},{3,1},{5,3},{7,5},{... | collective-permute-start | bytes 393224 | tf_op jit(solution)/shard_map/ppermute | solution.py:14
  62.5 5.5 %collective-permute-start.9 = (bf16[128,512]{0,1:T(8,128)(2,1)S(1)}, bf16[128,512]{0,1:T(8,128)(2,1)S(1)}, u32[]{:S(2)}, u32[]{:S(2)}) collective-permute-start(bf16[128,512]{0,1:T(8,128)(2,1)S(1)} %collective-permute-done.5), channel_id=1, source_target_pairs={{0,2},{2,4},{4,6},{6,8},{8,10},{10,12},{12,14},{1,3},{3,5},{5,7},{... | collective-permute-start | bytes 393224 | tf_op jit(solution)/shard_map/ppermute | solution.py:14
  69.6 4.8 %collective-permute-start.12 = (bf16[128,512]{0,1:T(8,128)(2,1)S(1)}, bf16[128,512]{0,1:T(8,128)(2,1)S(1)}, u32[]{:S(2)}, u32[]{:S(2)}) collective-permute-start(bf16[128,512]{0,1:T(8,128)(2,1)S(1)} %collective-permute-done.8), channel_id=1, source_target_pairs={{0,2},{2,4},{4,6},{6,8},{8,10},{10,12},{12,14},{1,3},{3,5},{5,7},{... | collective-permute-start | bytes 393224 | tf_op jit(solution)/shard_map/ppermute | solution.py:14
  74.9 1.3 %collective-permute-start.14 = (bf16[128,512]{0,1:T(8,128)(2,1)S(1)}, bf16[128,512]{0,1:T(8,128)(2,1)S(1)}, u32[]{:S(2)}, u32[]{:S(2)}) collective-permute-start(bf16[128,512]{0,1:T(8,128)(2,1)S(1)} %collective-permute-done.10), channel_id=1, source_target_pairs={{2,0},{4,2},{6,4},{8,6},{10,8},{12,10},{14,12},{3,1},{5,3},{7,5},{... | collective-permute-start | bytes 393224 | tf_op jit(solution)/shard_map/ppermute | solution.py:14
  76.2 1.3 %collective-permute-start.15 = (bf16[128,512]{0,1:T(8,128)(2,1)S(1)}, bf16[128,512]{0,1:T(8,128)(2,1)S(1)}, u32[]{:S(2)}, u32[]{:S(2)}) collective-permute-start(bf16[128,512]{0,1:T(8,128)(2,1)S(1)} %collective-permute-done.11), channel_id=1, source_target_pairs={{2,0},{4,2},{6,4},{8,6},{10,8},{12,10},{14,12},{3,1},{5,3},{7,5},{... | collective-permute-start | bytes 393224 | tf_op jit(solution)/shard_map/ppermute | solution.py:14
  77.5 5.4 %collective-permute-start.13 = (bf16[128,512]{0,1:T(8,128)(2,1)S(1)}, bf16[128,512]{0,1:T(8,128)(2,1)S(1)}, u32[]{:S(2)}, u32[]{:S(2)}) collective-permute-start(bf16[128,512]{0,1:T(8,128)(2,1)S(1)} %collective-permute-done.9), channel_id=1, source_target_pairs={{0,2},{2,4},{4,6},{6,8},{8,10},{10,12},{12,14},{1,3},{3,5},{5,7},{... | collective-permute-start | bytes 393224 | tf_op jit(solution)/shard_map/ppermute | solution.py:14
  84.8 1.4 %fusion.129 = f32[4,8,64,128]{3,2,1,0:T(8,128)S(1)} fusion(bf16[128,4,128,1]{0,2,3,1:T(8,128)(2,1)} %bitcast.85, f32[4,8,64,128]{3,2,1,0:T(8,128)S(1)} %get-tuple-element.100, f32[4,8,64]{2,1,0:T(8,128)S(1)} %get-tuple-element.21), kind=kOutput, calls=%fused_computation.166 | convolution fusion | flops 67633152 | bytes 2236416 | tf_op jit(solution)/shard_map/kgrn,nkd->kgrd/dot_general | solution.py:49
  88.1 1.4 %fusion.115 = f32[4,8,64,128]{3,2,1,0:T(8,128)S(1)} fusion(bf16[128,4,128,1]{0,2,3,1:T(8,128)(2,1)} %bitcast.85, f32[4,8,64,128]{3,2,1,0:T(8,128)S(1)} %get-tuple-element.80, f32[4,8,64]{2,1,0:T(8,128)S(1)} %get-tuple-element.40), kind=kOutput, calls=%fused_computation.162 | convolution fusion | flops 67633152 | bytes 2236416 | tf_op jit(solution)/shard_map/kgrn,nkd->kgrd/dot_general | solution.py:49
  92.9 0.7 fusion.100
  98.5 0.9 convolution_multiply_fusion.20
  104.1 1.1 fusion.59
  105.2 1.1 fusion.28
  106.3 1.1 fusion.56
  107.5 1.1 fusion.25
  108.7 1.1 fusion.49
  109.8 1.1 fusion.18
  111.0 1.1 fusion.42
  112.1 1.1 fusion.11
  113.8 1.0 fusion.64
  114.8 1.0 fusion.65
  115.9 0.7 copy.82
  116.6 1.3 %copy.83 = bf16[128,4096]{1,0:T(8,128)(2,1)} copy(bf16[128,4096]{0,1:T(8,128)(2,1)S(1)} %bitcast.243) | data formatting | bytes 2097152 | tf_op jit(solution)/shard_map/convert_element_type | solution.py:98
  (113 shorter events, 23.7 us)
Async XLA Ops:
  0.0 20.5 %copy-start.2 = (bf16[128,4096]{1,0:T(8,128)(2,1)S(1)}, bf16[128,4096]{1,0:T(8,128)(2,1)}, u32[]{:S(2)}) copy-start(bf16[128,4096]{1,0:T(8,128)(2,1)} %param.5) | copy-start | bytes 3145732
  1.7 34.0 %collective-permute-start = (bf16[128,512]{0,1:T(8,128)(2,1)}, bf16[128,512]{0,1:T(8,128)(2,1)}, u32[]{:S(2)}, u32[]{:S(2)}) collective-permute-start(bf16[128,512]{0,1:T(8,128)(2,1)} %copy.23), channel_id=1, source_target_pairs={{0,2},{2,4},{4,6},{6,8},{8,10},{10,12},{12,14},{1,3},{3,5},{5,7},{... | collective-permute-start | bytes 393224 | tf_op jit(solution)/shard_map/ppermute | solution.py:14
  7.2 25.4 %collective-permute-start.2 = (bf16[128,512]{0,1:T(8,128)(2,1)}, bf16[128,512]{0,1:T(8,128)(2,1)}, u32[]{:S(2)}, u32[]{:S(2)}) collective-permute-start(bf16[128,512]{0,1:T(8,128)(2,1)} %copy.23), channel_id=1, source_target_pairs={{2,0},{4,2},{6,4},{8,6},{10,8},{12,10},{14,12},{3,1},{5,3},{7,5},{... | collective-permute-start | bytes 393224 | tf_op jit(solution)/shard_map/ppermute | solution.py:14
  10.2 35.2 %collective-permute-start.3 = (bf16[128,512]{0,1:T(8,128)(2,1)}, bf16[128,512]{0,1:T(8,128)(2,1)}, u32[]{:S(2)}, u32[]{:S(2)}) collective-permute-start(bf16[128,512]{0,1:T(8,128)(2,1)} %copy.26), channel_id=1, source_target_pairs={{2,0},{4,2},{6,4},{8,6},{10,8},{12,10},{14,12},{3,1},{5,3},{7,5},{... | collective-permute-start | bytes 393224 | tf_op jit(solution)/shard_map/ppermute | solution.py:14
  11.5 35.3 %collective-permute-start.1 = (bf16[128,512]{0,1:T(8,128)(2,1)}, bf16[128,512]{0,1:T(8,128)(2,1)S(1)}, u32[]{:S(2)}, u32[]{:S(2)}) collective-permute-start(bf16[128,512]{0,1:T(8,128)(2,1)} %copy.26), channel_id=1, source_target_pairs={{0,2},{2,4},{4,6},{6,8},{8,10},{10,12},{12,14},{1,3},{3,5},{5,7},{... | collective-permute-start | bytes 393224 | tf_op jit(solution)/shard_map/ppermute | solution.py:14
  19.9 0.7 copy-start.19
  20.6 0.8 copy-start.5
  20.6 0.9 copy-start.6
  23.5 4.5 %copy-start.20 = (s32[128]{0:T(128)S(1)}, s32[128]{0:T(128)}, u32[]{:S(2)}) copy-start(s32[128]{0:T(128)} %copy-done.19) | copy-start | bytes 1540
  23.5 4.5 %copy-start.21 = (s32[128]{0:T(128)S(1)}, s32[128]{0:T(128)}, u32[]{:S(2)}) copy-start(s32[128]{0:T(128)} %get-tuple-element.113) | copy-start | bytes 1540
  23.6 5.9 %copy-start.4 = (bf16[128,4,128]{2,1,0:T(4,128)(2,1)S(1)}, bf16[128,4,128]{2,1,0:T(4,128)(2,1)}, u32[]{:S(2)}) copy-start(bf16[128,4,128]{2,1,0:T(4,128)(2,1)} %reshape.1671) | copy-start | bytes 393220
  28.0 4.2 %copy-start.3 = (f32[4,8,64]{2,1,0:T(8,128)S(1)}, f32[4,8,64]{2,1,0:T(8,128)}, u32[]{:S(2)}) copy-start(f32[4,8,64]{2,1,0:T(8,128)} %get-tuple-element.103) | copy-start | bytes 24580
  32.2 0.7 copy-start.15
  32.7 1.7 %copy-start.16 = (pred[64,128]{1,0:T(8,128)(4,1)S(1)}, pred[64,128]{1,0:T(8,128)(4,1)}, u32[]{:S(2)}) copy-start(pred[64,128]{1,0:T(8,128)(4,1)} %get-tuple-element.55) | copy-start | bytes 24580
  34.3 1.5 %copy-start.13 = (pred[64,128]{1,0:T(8,128)(4,1)S(1)}, pred[64,128]{1,0:T(8,128)(4,1)}, u32[]{:S(2)}) copy-start(pred[64,128]{1,0:T(8,128)(4,1)} %get-tuple-element.46) | copy-start | bytes 24580
  35.8 2.8 %copy-start.14 = (pred[64,128]{1,0:T(8,128)(4,1)S(1)}, pred[64,128]{1,0:T(8,128)(4,1)}, u32[]{:S(2)}) copy-start(pred[64,128]{1,0:T(8,128)(4,1)} %get-tuple-element.54) | copy-start | bytes 24580
  37.2 15.0 %copy-start.11 = (pred[64,128]{1,0:T(8,128)(4,1)S(1)}, pred[64,128]{1,0:T(8,128)(4,1)}, u32[]{:S(2)}) copy-start(pred[64,128]{1,0:T(8,128)(4,1)} %get-tuple-element.49) | copy-start | bytes 24580
  37.2 15.0 %collective-permute-start.6 = (bf16[128,512]{0,1:T(8,128)(2,1)}, bf16[128,512]{0,1:T(8,128)(2,1)S(1)}, u32[]{:S(2)}, u32[]{:S(2)}) collective-permute-start(bf16[128,512]{0,1:T(8,128)(2,1)} %collective-permute-done.2), channel_id=1, source_target_pairs={{2,0},{4,2},{6,4},{8,6},{10,8},{12,10},{14,12},{3,1},{5,3},{7,5},{... | collective-permute-start | bytes 393224 | tf_op jit(solution)/shard_map/ppermute | solution.py:14
  39.9 12.8 %copy-start.12 = (pred[64,128]{1,0:T(8,128)(4,1)S(1)}, pred[64,128]{1,0:T(8,128)(4,1)}, u32[]{:S(2)}) copy-start(pred[64,128]{1,0:T(8,128)(4,1)} %get-tuple-element.57) | copy-start | bytes 24580
  40.0 13.3 %collective-permute-start.4 = (bf16[128,512]{0,1:T(8,128)(2,1)}, bf16[128,512]{0,1:T(8,128)(2,1)S(1)}, u32[]{:S(2)}, u32[]{:S(2)}) collective-permute-start(bf16[128,512]{0,1:T(8,128)(2,1)} %collective-permute-done), channel_id=1, source_target_pairs={{0,2},{2,4},{4,6},{6,8},{8,10},{10,12},{12,14},{1,3},{3,5},{5,7},{... | collective-permute-start | bytes 393224 | tf_op jit(solution)/shard_map/ppermute | solution.py:14
  45.4 15.8 %collective-permute-start.7 = (bf16[128,512]{0,1:T(8,128)(2,1)}, bf16[128,512]{0,1:T(8,128)(2,1)S(1)}, u32[]{:S(2)}, u32[]{:S(2)}) collective-permute-start(bf16[128,512]{0,1:T(8,128)(2,1)} %collective-permute-done.3), channel_id=1, source_target_pairs={{2,0},{4,2},{6,4},{8,6},{10,8},{12,10},{14,12},{3,1},{5,3},{7,5},{... | collective-permute-start | bytes 393224 | tf_op jit(solution)/shard_map/ppermute | solution.py:14
  46.7 15.8 %collective-permute-start.5 = (bf16[128,512]{0,1:T(8,128)(2,1)S(1)}, bf16[128,512]{0,1:T(8,128)(2,1)S(1)}, u32[]{:S(2)}, u32[]{:S(2)}) collective-permute-start(bf16[128,512]{0,1:T(8,128)(2,1)S(1)} %collective-permute-done.1), channel_id=1, source_target_pairs={{0,2},{2,4},{4,6},{6,8},{8,10},{10,12},{12,14},{1,3},{3,5},{5,7},{... | collective-permute-start | bytes 393224 | tf_op jit(solution)/shard_map/ppermute | solution.py:14
  52.7 0.7 copy-start.9
  53.3 2.0 %copy-start.10 = (pred[64,128]{1,0:T(8,128)(4,1)S(1)}, pred[64,128]{1,0:T(8,128)(4,1)}, u32[]{:S(2)}) copy-start(pred[64,128]{1,0:T(8,128)(4,1)} %get-tuple-element.56) | copy-start | bytes 24580
  53.9 14.1 %collective-permute-start.10 = (bf16[128,512]{0,1:T(8,128)(2,1)S(1)}, bf16[128,512]{0,1:T(8,128)(2,1)S(1)}, u32[]{:S(2)}, u32[]{:S(2)}) collective-permute-start(bf16[128,512]{0,1:T(8,128)(2,1)S(1)} %collective-permute-done.6), channel_id=1, source_target_pairs={{2,0},{4,2},{6,4},{8,6},{10,8},{12,10},{14,12},{3,1},{5,3},{7,5},{... | collective-permute-start | bytes 393224 | tf_op jit(solution)/shard_map/ppermute | solution.py:14
  55.8 12.8 %copy-start.8 = (pred[64,128]{1,0:T(8,128)(4,1)S(1)}, pred[64,128]{1,0:T(8,128)(4,1)}, u32[]{:S(2)}) copy-start(pred[64,128]{1,0:T(8,128)(4,1)} %get-tuple-element.59) | copy-start | bytes 24580
  55.8 13.3 %collective-permute-start.8 = (bf16[128,512]{0,1:T(8,128)(2,1)S(1)}, bf16[128,512]{0,1:T(8,128)(2,1)S(1)}, u32[]{:S(2)}, u32[]{:S(2)}) collective-permute-start(bf16[128,512]{0,1:T(8,128)(2,1)S(1)} %collective-permute-done.4), channel_id=1, source_target_pairs={{0,2},{2,4},{4,6},{6,8},{8,10},{10,12},{12,14},{1,3},{3,5},{5,7},{... | collective-permute-start | bytes 393224 | tf_op jit(solution)/shard_map/ppermute | solution.py:14
  61.2 15.0 %collective-permute-start.11 = (bf16[128,512]{0,1:T(8,128)(2,1)S(1)}, bf16[128,512]{0,1:T(8,128)(2,1)S(1)}, u32[]{:S(2)}, u32[]{:S(2)}) collective-permute-start(bf16[128,512]{0,1:T(8,128)(2,1)S(1)} %collective-permute-done.7), channel_id=1, source_target_pairs={{2,0},{4,2},{6,4},{8,6},{10,8},{12,10},{14,12},{3,1},{5,3},{7,5},{... | collective-permute-start | bytes 393224 | tf_op jit(solution)/shard_map/ppermute | solution.py:14
  62.5 15.0 %collective-permute-start.9 = (bf16[128,512]{0,1:T(8,128)(2,1)S(1)}, bf16[128,512]{0,1:T(8,128)(2,1)S(1)}, u32[]{:S(2)}, u32[]{:S(2)}) collective-permute-start(bf16[128,512]{0,1:T(8,128)(2,1)S(1)} %collective-permute-done.5), channel_id=1, source_target_pairs={{0,2},{2,4},{4,6},{6,8},{8,10},{10,12},{12,14},{1,3},{3,5},{5,7},{... | collective-permute-start | bytes 393224 | tf_op jit(solution)/shard_map/ppermute | solution.py:14
  69.6 13.3 %collective-permute-start.12 = (bf16[128,512]{0,1:T(8,128)(2,1)S(1)}, bf16[128,512]{0,1:T(8,128)(2,1)S(1)}, u32[]{:S(2)}, u32[]{:S(2)}) collective-permute-start(bf16[128,512]{0,1:T(8,128)(2,1)S(1)} %collective-permute-done.8), channel_id=1, source_target_pairs={{0,2},{2,4},{4,6},{6,8},{8,10},{10,12},{12,14},{1,3},{3,5},{5,7},{... | collective-permute-start | bytes 393224 | tf_op jit(solution)/shard_map/ppermute | solution.py:14
  74.9 8.5 %collective-permute-start.14 = (bf16[128,512]{0,1:T(8,128)(2,1)S(1)}, bf16[128,512]{0,1:T(8,128)(2,1)S(1)}, u32[]{:S(2)}, u32[]{:S(2)}) collective-permute-start(bf16[128,512]{0,1:T(8,128)(2,1)S(1)} %collective-permute-done.10), channel_id=1, source_target_pairs={{2,0},{4,2},{6,4},{8,6},{10,8},{12,10},{14,12},{3,1},{5,3},{7,5},{... | collective-permute-start | bytes 393224 | tf_op jit(solution)/shard_map/ppermute | solution.py:14
  76.2 18.4 %collective-permute-start.15 = (bf16[128,512]{0,1:T(8,128)(2,1)S(1)}, bf16[128,512]{0,1:T(8,128)(2,1)S(1)}, u32[]{:S(2)}, u32[]{:S(2)}) collective-permute-start(bf16[128,512]{0,1:T(8,128)(2,1)S(1)} %collective-permute-done.11), channel_id=1, source_target_pairs={{2,0},{4,2},{6,4},{8,6},{10,8},{12,10},{14,12},{3,1},{5,3},{7,5},{... | collective-permute-start | bytes 393224 | tf_op jit(solution)/shard_map/ppermute | solution.py:14
  77.5 36.2 %collective-permute-start.13 = (bf16[128,512]{0,1:T(8,128)(2,1)S(1)}, bf16[128,512]{0,1:T(8,128)(2,1)S(1)}, u32[]{:S(2)}, u32[]{:S(2)}) collective-permute-start(bf16[128,512]{0,1:T(8,128)(2,1)S(1)} %collective-permute-done.9), channel_id=1, source_target_pairs={{0,2},{2,4},{4,6},{6,8},{8,10},{10,12},{12,14},{1,3},{3,5},{5,7},{... | collective-permute-start | bytes 393224 | tf_op jit(solution)/shard_map/ppermute | solution.py:14
  83.4 0.7 copy-start.18
  84.8 1.4 %copy-start.7 = (pred[64,128]{1,0:T(8,128)(4,1)S(1)}, pred[64,128]{1,0:T(8,128)(4,1)}, u32[]{:S(2)}) copy-start(pred[64,128]{1,0:T(8,128)(4,1)} %get-tuple-element.60) | copy-start | bytes 24580
  86.7 0.7 copy-start.17
  96.5 1.3 %copy-start = (f32[4,8,64,128]{3,2,1,0:T(8,128)S(1)}, f32[4,8,64,128]{3,2,1,0:T(8,128)}, u32[]{:S(2)}) copy-start(f32[4,8,64,128]{3,2,1,0:T(8,128)} %get-tuple-element.106) | copy-start | bytes 3145732
  101.4 1.3 %copy-start.1 = (f32[4,8,64,128]{3,2,1,0:T(8,128)S(1)}, f32[4,8,64,128]{3,2,1,0:T(8,128)}, u32[]{:S(2)}) copy-start(f32[4,8,64,128]{3,2,1,0:T(8,128)} %get-tuple-element.86) | copy-start | bytes 3145732
where the time goes:
time: 119 us; the launch traced here: 118 us
  starting transfers between devices  53 us (45%)
  matrix products  36.7 us (31%)
  other arithmetic  17.3 us (15%)
  local copies, waits for them, and re-layouts  9.79 us (8%)
    ppermute x16, starting transfers between devices, passed_along(): lax.ppermute(value, axis, [(source, source + steps) for source in range(l...  53 us
    dot_general x18, matrix products, absorb(): jnp.einsum('kgrn,nkd->kgrd', exps.astype(jnp.bfloat16), value_tile, prefe...  16.7 us
    dot_general x18, matrix products, absorb(): jnp.einsum('rkgd,nkd->kgrn', query_part, key_tile, preferred_element_type...  16.6 us
    reduce_sum x18, other arithmetic, absorb(): total = total * factor + jnp.sum(exps, axis=-1)  11.7 us
    unnamed x49, local copies, waits for them, and re-layouts  5.24 us
    and x3, other arithmetic, visit_block(): present & (key_positions[None, :] <= half_positions[:, None])  3.68 us
  transfers between devices with their start and end apart: 16, of which 0 were waited for; matrix products, arithmetic and copies ran while one was open for 48% of the time, Pallas kernels for 0%

commit v1 on v0

v1 whole, which is shorter than its diff:
```python
import functools

import jax
import jax.numpy as jnp
from jax import lax
from jax.experimental import pallas as pl
from jax.experimental.pallas import tpu as pltpu
from jax.sharding import PartitionSpec as P

HD = 128
GQ = 8
WINDOW = 256
LOG2E = 1.4426950408889634
MESH = pl.DeviceIdType.MESH


def kernel(
    slots, inner, heads, half, reach, prefix,
    q_hbm, k_hbm, v_hbm, pk_hbm, pv_hbm, o_hbm,
    q_v, kv, pre, o_v, q_sem, kv_sem, pre_sem, o_sem, send_sem, recv_sem,
):
    me = lax.axis_index("outer") * inner + lax.axis_index("inner")
    width = GQ * HD

    def load_kv(b, h, which):
        ref = (k_hbm, v_hbm)[which]
        return pltpu.make_async_copy(
            ref.at[pl.ds(b * half, half), pl.ds(h * HD, HD)],
            kv.at[b * (reach + 1), h, which],
            kv_sem.at[b, h, which],
        )

    def load_pre(h, which):
        ref = (pk_hbm, pv_hbm)[which]
        return pltpu.make_async_copy(ref.at[:, pl.ds(h * HD, HD)], pre.at[h, which], pre_sem.at[h, which])

    def load_q(h):
        return pltpu.make_async_copy(q_hbm.at[:, pl.ds(h * width, width)], q_v.at[h], q_sem.at[h])

    def store_o(h):
        return pltpu.make_async_copy(o_v.at[h], o_hbm.at[:, pl.ds(h * width, width)], o_sem.at[h])

    for h in range(heads):
        for b in range(2):
            for which in range(2):
                load_kv(b, h, which).start()
    for h in range(heads):
        load_q(h).start()
        load_pre(h, 0).start()
        load_pre(h, 1).start()

    sends = []
    for d in range(1, reach + 1):
        sends.append((me + d < slots, me + d, 0, d))
        sends.append((me - d >= 0, me - d, 1, reach + 1 + d))
        back = 2 * slots - 1 - me - d
        sends.append((back < me, back, 0, reach + 1 + d))
    receives = []
    for d in range(1, reach + 1):
        receives.append((me - d >= 0, me - d, d))
        receives.append((me + d < slots, me + d, reach + 1 + d))
        fold = 2 * slots - 1 - me - d
        receives.append(((fold > me) & (me + d >= slots), fold, reach + 1 + d))

    def place(slot):
        return {"outer": slot // inner, "inner": slot % inner}

    barrier = pltpu.get_barrier_semaphore()
    count = jnp.int32(0)
    for d in range(1, reach + 1):
        for valid, other in ((me + d < slots, me + d), (me - d >= 0, me - d)):
            count = count + valid.astype(jnp.int32)

            @pl.when(valid)
            def _():
                pl.semaphore_signal(barrier, inc=1, device_id=place(other), device_id_type=MESH)

    pl.semaphore_wait(barrier, count)

    def send(h, n):
        valid, partner, b, index = sends[n]
        return pltpu.make_async_remote_copy(
            src_ref=kv.at[b * (reach + 1), h],
            dst_ref=kv.at[index, h],
            send_sem=send_sem.at[h, n],
            recv_sem=recv_sem.at[h, index],
            device_id=place(partner),
            device_id_type=MESH,
        )

    for h in range(heads):
        for b in range(2):
            for which in range(2):
                load_kv(b, h, which).wait()
        for n in range(len(sends)):

            @pl.when(sends[n][0])
            def _():
                send(h, n).start()

    rows = lax.broadcasted_iota(jnp.int32, (half, half), 0)
    cols = lax.broadcasted_iota(jnp.int32, (half, half), 1)
    low = jnp.float32(-jnp.inf)
    causal = jnp.where(cols <= rows, 0.0, low)
    farthest = jnp.where(cols > rows, 0.0, low)

    def attend(h, b, blocks, biases):
        query = jnp.concatenate(
            [q_v[h, b * half : (b + 1) * half, g * HD : (g + 1) * HD] for g in range(GQ)], axis=0
        )
        keys = jnp.concatenate([pre[h, 0]] + [kv[i, h, 0] for i in blocks], axis=0)
        vals = jnp.concatenate([pre[h, 1]] + [kv[i, h, 1] for i in blocks], axis=0)
        vals = jnp.concatenate([vals, jnp.ones_like(vals)], axis=1)
        scores = lax.dot_general(query, keys, (((1,), (1,)), ((), ())), preferred_element_type=jnp.float32)
        scores = scores * (LOG2E / HD**0.5)
        bias = jnp.concatenate([jnp.zeros((half, prefix), jnp.float32)] + biases, axis=1)
        scores = (scores.reshape(GQ, half, -1) + bias[None]).reshape(GQ * half, -1)
        top = jnp.max(scores, axis=1, keepdims=True)
        weights = jnp.exp2(scores - top).astype(jnp.bfloat16)
        both = jnp.dot(weights, vals, preferred_element_type=jnp.float32)
        out = (both[:, :HD] / both[:, HD:]).astype(jnp.bfloat16)
        for g in range(GQ):
            o_v[h, b * half : (b + 1) * half, g * HD : (g + 1) * HD] = out[g * half : (g + 1) * half]

    def head(h, carry):
        load_q(h).wait()
        load_pre(h, 0).wait()
        load_pre(h, 1).wait()
        for valid, partner, index in receives:

            @pl.when(valid)
            def _():
                pltpu.make_async_remote_copy(
                    src_ref=kv.at[0, h],
                    dst_ref=kv.at[index, h],
                    send_sem=send_sem.at[h, 0],
                    recv_sem=recv_sem.at[h, index],
                    device_id=place(partner),
                    device_id_type=MESH,
                ).wait_recv()

        zero = jnp.zeros((half, half), jnp.float32)
        blocks, biases = [0], [causal]
        for d in range(1, reach + 1):
            there = me - d >= 0
            blocks.append(jnp.where(there, d, 0))
            biases.append(jnp.where(there, farthest if d == reach else zero, low))
        attend(h, 0, blocks, biases)
        blocks, biases = [reach + 1], [causal]
        for d in range(1, reach + 1):
            fold = 2 * slots - 1 - me - d
            blocks.append(jnp.where(fold <= me, me - fold, reach + 1 + d))
            biases.append(farthest if d == reach else zero)
        attend(h, 1, blocks, biases)
        store_o(h).start()
        return carry

    lax.fori_loop(0, heads, head, 0)
    for h in range(heads):
        store_o(h).wait()
        for n in range(len(sends)):

            @pl.when(sends[n][0])
            def _():
                send(h, n).wait_send()


def solution(mesh):
    inner = mesh.shape["inner"]
    slots = mesh.shape["outer"] * inner

    def local(q, k, v, pk, pv):
        rows, columns = k.shape
        heads, half, prefix = columns // HD, rows // 2, pk.shape[0]
        reach = WINDOW // half
        any_spec = pl.BlockSpec(memory_space=pl.ANY)
        scores = q.shape[0] * heads * GQ * (prefix + (reach + 1) * half)
        return pl.pallas_call(
            functools.partial(kernel, slots, inner, heads, half, reach, prefix),
            out_shape=jax.ShapeDtypeStruct(q.shape, jnp.bfloat16),
            in_specs=[any_spec] * 5,
            out_specs=any_spec,
            scratch_shapes=[
                pltpu.VMEM((heads, rows, GQ * HD), jnp.bfloat16),
                pltpu.VMEM((2 * (reach + 1), heads, 2, half, HD), jnp.bfloat16),
                pltpu.VMEM((heads, 2, prefix, HD), jnp.bfloat16),
                pltpu.VMEM((heads, rows, GQ * HD), jnp.bfloat16),
                pltpu.SemaphoreType.DMA((heads,)),
                pltpu.SemaphoreType.DMA((2, heads, 2)),
                pltpu.SemaphoreType.DMA((heads, 2)),
                pltpu.SemaphoreType.DMA((heads,)),
                pltpu.SemaphoreType.DMA((heads, 3 * reach)),
                pltpu.SemaphoreType.DMA((heads, 2 * (reach + 1))),
            ],
            compiler_params=pltpu.CompilerParams(
                collective_id=0, has_side_effects=True, vmem_limit_bytes=32 * 1024 * 1024
            ),
            cost_estimate=pl.CostEstimate(
                flops=scores * HD * 4, bytes_accessed=4 * q.size, transcendentals=scores
            ),
        )(q, k, v, pk, pv)

    placed = (
        P(("groups", "outer", "inner"), "heads"),
        P(("groups", "outer", "inner"), "heads"),
        P(("groups", "outer", "inner"), "heads"),
        P("groups", "heads"),
        P("groups", "heads"),
    )
    return jax.shard_map(
        local,
        mesh=mesh,
        in_specs=placed,
        out_specs=P(("groups", "outer", "inner"), "heads"),
        check_vma=False,
    )
```

time: 119 us -> 32.1 us (0.27)
  starting transfers between devices: 53 us -> 0 us
  matrix products: 36.7 us -> 0 us
  Pallas kernels: 0 us -> 26.1 us
  other arithmetic: 17.3 us -> 0 us
  local copies, waits for them, and re-layouts: 9.79 us -> 5.68 us
    ppermute x16 -> x0, starting transfers between devices: 53 us -> none  [passed_along(): lax.ppermute(value, axis, [(source, source + steps) for source in range(l...]
    dot_general x40 -> x0, matrix products: 36.7 us -> none  [the longest x18 16.7 us: absorb(): jnp.einsum('kgrn,nkd->kgrd', exps.astype(jnp.bfloat16), value_tile, prefe...]
    pallas_call x0 -> x1, Pallas kernels: none -> 26.1 us  [local(): pl.pallas_call(functools.partial(kernel, slots, inner, heads, half, reach...]
    reduce_sum x20 -> x0, other arithmetic: 12.1 us -> none  [the longest x18 11.7 us: absorb(): total = total * factor + jnp.sum(exps, axis=-1)]
    and x3 -> x0, other arithmetic: 3.68 us -> none  [visit_block(): present & (key_positions[None, :] <= half_positions[:, None])]
    reshape x4 -> x0, local copies, waits for them, and re-layouts: 2.57 us -> none  [the longest x1 1.6 us: visit_block(): key_grid = block_keys.reshape(row_count, kv_heads, HD)]
    convert_element_type x2 -> x0, local copies, waits for them, and re-layouts: 1.98 us -> none  [local(): joined.transpose(2, 0, 1, 3).reshape(row_count, kv_heads * GQ * HD)]
    unnamed x49 -> x11, local copies, waits for them, and re-layouts: 5.24 us -> 5.68 us
  transfers between devices with their start and end apart: 16 -> 0, of which waited for: 0 -> 0; matrix products, arithmetic and copies ran while one was open for 48% -> 0% of each run, Pallas kernels for 0% -> 0%
where the time goes in v1:
time: 32.1 us; the launch traced here: 31.8 us
  Pallas kernels  26.1 us (81%)
  local copies, waits for them, and re-layouts  5.68 us (18%)
    pallas_call x1, Pallas kernels, local(): pl.pallas_call(functools.partial(kernel, slots, inner, heads, half, reach...  26.1 us
    unnamed x11, local copies, waits for them, and re-layouts  5.68 us

profile of v1, /device:TPU:0, one launch (start us, length us, event | category | flops | bytes accessed | tf_op | source)
XLA Modules:
  0.0 31.8 jit_solution(16424240573279924768)
XLA Ops:
  0.0 0.0 copy-start
  0.0 1.2 %copy-done = bf16[128,4096]{1,0:T(8,128)(2,1)S(1)} copy-done((bf16[128,4096]{1,0:T(8,128)(2,1)S(1)}, bf16[128,4096]{1,0:T(8,128)(2,1)}, u32[]{:S(2)}) %copy-start) | copy-done | bytes 1048600
  1.2 0.0 copy-start.1
  1.2 0.9 %copy-done.1 = bf16[128,512]{1,0:T(8,128)(2,1)S(1)} copy-done((bf16[128,512]{1,0:T(8,128)(2,1)S(1)}, bf16[128,512]{1,0:T(8,128)(2,1)}, u32[]{:S(2)}) %copy-start.1) | copy-done | bytes 131096
  2.1 0.0 copy-start.2
  2.1 0.9 %copy-done.2 = bf16[128,512]{1,0:T(8,128)(2,1)S(1)} copy-done((bf16[128,512]{1,0:T(8,128)(2,1)S(1)}, bf16[128,512]{1,0:T(8,128)(2,1)}, u32[]{:S(2)}) %copy-start.2) | copy-done | bytes 131096
  3.0 0.0 copy-start.3
  3.0 0.8 %copy-done.3 = bf16[64,512]{1,0:T(8,128)(2,1)S(1)} copy-done((bf16[64,512]{1,0:T(8,128)(2,1)S(1)}, bf16[64,512]{1,0:T(8,128)(2,1)}, u32[]{:S(2)}) %copy-start.3) | copy-done | bytes 65560
  3.9 0.0 copy-start.4
  3.9 0.8 %copy-done.4 = bf16[64,512]{1,0:T(8,128)(2,1)S(1)} copy-done((bf16[64,512]{1,0:T(8,128)(2,1)S(1)}, bf16[64,512]{1,0:T(8,128)(2,1)}, u32[]{:S(2)}) %copy-start.4) | copy-done | bytes 65560
  4.7 26.1 %shard_map.55 = bf16[128,4096]{1,0:T(8,128)(2,1)S(1)} custom-call(bf16[128,4096]{1,0:T(8,128)(2,1)S(1)} %copy-done, bf16[128,512]{1,0:T(8,128)(2,1)S(1)} %copy-done.1, bf16[128,512]{1,0:T(8,128)(2,1)S(1)} %copy-done.2, bf16[64,512]{1,0:T(8,128)(2,1)S(1)} %copy-done.3, bf16[64,512]{1,0:T(8,128)(2,1)S(1)} %copy-done.4), custom_call_target="tpu_custom_call" | custom-call | flops 805306368 | bytes 2097152 | tf_op jit(solution)/shard_map/pallas_call | solution.py:178
  30.9 1.0 %copy.7 = bf16[128,4096]{1,0:T(8,128)(2,1)} copy(bf16[128,4096]{1,0:T(8,128)(2,1)S(1)} %shard_map.55) | data formatting | bytes 2097152
Async XLA Ops:
  0.0 1.2 %copy-start = (bf16[128,4096]{1,0:T(8,128)(2,1)S(1)}, bf16[128,4096]{1,0:T(8,128)(2,1)}, u32[]{:S(2)}) copy-start(bf16[128,4096]{1,0:T(8,128)(2,1)} %q_hbm.1) | copy-start | bytes 3145732
  1.2 0.9 %copy-start.1 = (bf16[128,512]{1,0:T(8,128)(2,1)S(1)}, bf16[128,512]{1,0:T(8,128)(2,1)}, u32[]{:S(2)}) copy-start(bf16[128,512]{1,0:T(8,128)(2,1)} %k_hbm.1) | copy-start | bytes 393220
  2.1 0.9 %copy-start.2 = (bf16[128,512]{1,0:T(8,128)(2,1)S(1)}, bf16[128,512]{1,0:T(8,128)(2,1)}, u32[]{:S(2)}) copy-start(bf16[128,512]{1,0:T(8,128)(2,1)} %v_hbm.1) | copy-start | bytes 393220
  3.0 0.8 %copy-start.3 = (bf16[64,512]{1,0:T(8,128)(2,1)S(1)}, bf16[64,512]{1,0:T(8,128)(2,1)}, u32[]{:S(2)}) copy-start(bf16[64,512]{1,0:T(8,128)(2,1)} %pk_hbm.1) | copy-start | bytes 196612
  3.9 0.8 %copy-start.4 = (bf16[64,512]{1,0:T(8,128)(2,1)S(1)}, bf16[64,512]{1,0:T(8,128)(2,1)}, u32[]{:S(2)}) copy-start(bf16[64,512]{1,0:T(8,128)(2,1)} %pv_hbm.1) | copy-start | bytes 196612

commit v2 on v1

--- a/solution.py
+++ b/solution.py
@@ -12,6 +12,79 @@
 WINDOW = 256
 LOG2E = 1.4426950408889634
 MESH = pl.DeviceIdType.MESH
+
+TREES = {
+    (0, 0): ((0, 2), (0, 1), (2, 4), (1, 3)),
+    (1, 0): ((1, 3), (3, 5), (3, 2), (2, 4)),
+    (1, 1): ((1, 0),),
+    (2, 0): ((2, 4), (2, 3), (4, 6), (3, 5)),
+    (2, 1): ((2, 0), (0, 1)),
+    (3, 0): ((3, 5), (5, 7), (5, 4), (4, 6)),
+    (3, 1): ((3, 1), (1, 0), (0, 2)),
+    (4, 0): ((4, 6), (4, 5), (6, 7)),
+    (4, 1): ((4, 2), (2, 0), (2, 3), (0, 1)),
+    (5, 0): ((5, 7), (7, 6)),
+    (5, 1): ((5, 3), (5, 4), (3, 1), (3, 2)),
+    (6, 0): ((6, 7), (7, 5)),
+    (6, 1): ((6, 4), (4, 2), (4, 5), (2, 3)),
+    (7, 0): ((7, 5), (7, 6), (5, 4)),
+    (7, 1): ((7, 5), (7, 6), (5, 3), (6, 4)),
+}
+
+
+class Route:
+    def __init__(self, here):
+        self.here = here
+        self.own, self.relays, self.leaves, self.sends, self.partners = [], [], [], [], []
+
+    def send(self, valid, source, partner, index):
+        self.sends.append((valid, len(self.sends), source, partner, index))
+        return self.sends[-1]
+
+
+def programs(slots, inner, reach, me):
+    def landing(slot, half, at):
+        if slot == at:
+            return half * (reach + 1)
+        if half == 1:
+            return reach + 1 + slot - at
+        return at - slot if slot < at else reach + 1 + 2 * slots - 1 - at - slot
+
+    if (slots, inner, reach) == (8, 2, 4):
+        routes = []
+        for at in range(slots):
+            route = Route(me == at)
+            depths = []
+            for (slot, half), hops in TREES.items():
+                depth = {slot: 0}
+                for a, b in hops:
+                    depth[b] = depth[a] + 1
+                    for other in (a, b):
+                        if at in (a, b) and other != at and (None, other) not in route.partners:
+                            route.partners.append((None, other))
+                index = landing(slot, half, at)
+                sends = [route.send(None, index, b, landing(slot, half, b)) for a, b in hops if a == at]
+                if slot == at:
+                    route.own.extend(sends)
+                elif at in depth and sends:
+                    depths.append((depth[at], index, sends))
+                elif at in depth:
+                    route.leaves.append((None, index))
+            route.relays = depths
+            routes.append(route)
+        return routes
+
+    route = Route(None)
+    for d in range(1, reach + 1):
+        up, down = (me + d < slots, me + d), (me - d >= 0, me - d)
+        route.partners += [up, down]
+        route.own.append(route.send(*up[:1], 0, up[1], d))
+        route.own.append(route.send(*down[:1], reach + 1, down[1], reach + 1 + d))
+        route.leaves.append((down[0], d))
+        fold = 2 * slots - 1 - me - d
+        route.own.append(route.send(fold < me, 0, fold, reach + 1 + d))
+        route.leaves.append((up[0] | (fold > me), reach + 1 + d))
+    return [route]
 
 
 def kernel(
@@ -49,38 +122,20 @@
         load_pre(h, 0).start()
         load_pre(h, 1).start()
 
-    sends = []
-    for d in range(1, reach + 1):
-        sends.append((me + d < slots, me + d, 0, d))
-        sends.append((me - d >= 0, me - d, 1, reach + 1 + d))
-        back = 2 * slots - 1 - me - d
-        sends.append((back < me, back, 0, reach + 1 + d))
-    receives = []
-    for d in range(1, reach + 1):
-        receives.append((me - d >= 0, me - d, d))
-        receives.append((me + d < slots, me + d, reach + 1 + d))
-        fold = 2 * slots - 1 - me - d
-        receives.append(((fold > me) & (me + d >= slots), fold, reach + 1 + d))
+    routes = programs(slots, inner, reach, me)
 
     def place(slot):
         return {"outer": slot // inner, "inner": slot % inner}
 
-    barrier = pltpu.get_barrier_semaphore()
-    count = jnp.int32(0)
-    for d in range(1, reach + 1):
-        for valid, other in ((me + d < slots, me + d), (me - d >= 0, me - d)):
-            count = count + valid.astype(jnp.int32)
-
-            @pl.when(valid)
-            def _():
-                pl.semaphore_signal(barrier, inc=1, device_id=place(other), device_id_type=MESH)
-
-    pl.semaphore_wait(barrier, count)
-
-    def send(h, n):
-        valid, partner, b, index = sends[n]
+    def when(condition, body):
+        if condition is None:
+            body()
+        else:
+            pl.when(condition)(body)
+
+    def copy(h, n, source, partner, index):
         return pltpu.make_async_remote_copy(
-            src_ref=kv.at[b * (reach + 1), h],
+            src_ref=kv.at[source, h],
             dst_ref=kv.at[index, h],
             send_sem=send_sem.at[h, n],
             recv_sem=recv_sem.at[h, index],
@@ -88,15 +143,61 @@
             device_id_type=MESH,
         )
 
-    for h in range(heads):
+    def start(h, sends):
+        for valid, n, source, partner, index in sends:
+            when(valid, lambda: copy(h, n, source, partner, index).start())
+
+    def arrived(h, valid, index):
+        when(valid, lambda: copy(h, 0, 0, 0, index).wait_recv())
+
+    def greet(route):
+        barrier = pltpu.get_barrier_semaphore()
+        count = 0
+        for valid, other in route.partners:
+            count = count + (1 if valid is None else valid.astype(jnp.int32))
+            when(
+                valid,
+                lambda: pl.semaphore_signal(barrier, inc=1, device_id=place(other), device_id_type=MESH),
+            )
+        pl.semaphore_wait(barrier, count)
+
+    def each_route(body):
+        for route in routes:
+            when(route.here, lambda: body(route))
+
+    each_route(greet)
+
+    def own(h):
         for b in range(2):
             for which in range(2):
                 load_kv(b, h, which).wait()
-        for n in range(len(sends)):
-
-            @pl.when(sends[n][0])
-            def _():
-                send(h, n).start()
+        each_route(lambda route: start(h, route.own))
+
+    def relay(h, level):
+        def body(route):
+            for depth, index, sends in route.relays:
+                if depth == level:
+                    arrived(h, None, index)
+                    start(h, sends)
+
+        each_route(body)
+
+    def leaves(h):
+        def body(route):
+            for valid, index in route.leaves:
+                arrived(h, valid, index)
+
+        each_route(body)
+
+    def drain(h):
+        def body(route):
+            for valid, n, source, partner, index in route.sends:
+                when(valid, lambda: copy(h, n, source, partner, index).wait_send())
+
+        each_route(body)
+
+    for h in range(heads):
+        own(h)
 
     rows = lax.broadcasted_iota(jnp.int32, (half, half), 0)
     cols = lax.broadcasted_iota(jnp.int32, (half, half), 1)
@@ -120,24 +221,13 @@
         both = jnp.dot(weights, vals, preferred_element_type=jnp.float32)
         out = (both[:, :HD] / both[:, HD:]).astype(jnp.bfloat16)
         for g in range(GQ):
-            o_v[h, b * half : (b + 1) * half, g * HD : (g + 1) * HD] = out[g * half : (g + 1) * half]
-
-    def head(h, carry):
+            o_hbm[b * half : (b + 1) * half, pl.ds(pl.multiple_of(h * width + g * HD, HD), HD)] = out[g * half : (g + 1) * half]
+
+    def head(h):
         load_q(h).wait()
         load_pre(h, 0).wait()
         load_pre(h, 1).wait()
-        for valid, partner, index in receives:
-
-            @pl.when(valid)
-            def _():
-                pltpu.make_async_remote_copy(
-                    src_ref=kv.at[0, h],
-                    dst_ref=kv.at[index, h],
-                    send_sem=send_sem.at[h, 0],
-                    recv_sem=recv_sem.at[h, index],
-                    device_id=place(partner),
-                    device_id_type=MESH,
-                ).wait_recv()
+        leaves(h)
 
         zero = jnp.zeros((half, half), jnp.float32)
         blocks, biases = [0], [causal]
@@ -152,17 +242,25 @@
             blocks.append(jnp.where(fold <= me, me - fold, reach + 1 + d))
             biases.append(farthest if d == reach else zero)
         attend(h, 1, blocks, biases)
-        store_o(h).start()
+
+    def step(h, carry):
+        @pl.when(h < heads)
+        def _():
+            relay(h, 1)
+
+        @pl.when((h >= 1) & (h <= heads))
+        def _():
+            relay(h - 1, 2)
+
+        @pl.when(h >= 2)
+        def _():
+            head(h - 2)
+
         return carry
 
-    lax.fori_loop(0, heads, head, 0)
+    lax.fori_loop(0, heads + 2, step, 0)
     for h in range(heads):
-        store_o(h).wait()
-        for n in range(len(sends)):
-
-            @pl.when(sends[n][0])
-            def _():
-                send(h, n).wait_send()
+        drain(h)
 
 
 def solution(mesh):
@@ -177,9 +275,9 @@
         scores = q.shape[0] * heads * GQ * (prefix + (reach + 1) * half)
         return pl.pallas_call(
             functools.partial(kernel, slots, inner, heads, half, reach, prefix),
-            out_shape=jax.ShapeDtypeStruct(q.shape, jnp.bfloat16),
+            out_shape=pltpu.VMEM(q.shape, jnp.bfloat16),
             in_specs=[any_spec] * 5,
-            out_specs=any_spec,
+            out_specs=pl.BlockSpec(memory_space=pltpu.VMEM),
             scratch_shapes=[
                 pltpu.VMEM((heads, rows, GQ * HD), jnp.bfloat16),
                 pltpu.VMEM((2 * (reach + 1), heads, 2, half, HD), jnp.bfloat16),
@@ -193,7 +291,7 @@
                 pltpu.SemaphoreType.DMA((heads, 2 * (reach + 1))),
             ],
             compiler_params=pltpu.CompilerParams(
-                collective_id=0, has_side_effects=True, vmem_limit_bytes=32 * 1024 * 1024
+                collective_id=0, has_side_effects=True, vmem_limit_bytes=58 * 1024 * 1024
             ),
             cost_estimate=pl.CostEstimate(
                 flops=scores * HD * 4, bytes_accessed=4 * q.size, transcendentals=scores

time: 32.1 us -> 21.7 us (0.68)
  Pallas kernels: 26.1 us -> 20.6 us
  local copies, waits for them, and re-layouts: 5.68 us -> 0.97 us
    pallas_call x1, Pallas kernels: 26.1 us -> 20.6 us  [local(): pl.pallas_call(functools.partial(kernel, slots, inner, heads, half, reach...]
    unnamed x11 -> x1, local copies, waits for them, and re-layouts: 5.68 us -> 0.97 us
where the time goes in v2:
time: 21.7 us; the launch traced here: 21.5 us
  Pallas kernels  20.6 us (95%)
  local copies, waits for them, and re-layouts  0.97 us (4%)
    pallas_call x1, Pallas kernels, local(): pl.pallas_call(functools.partial(kernel, slots, inner, heads, half, reach...  20.6 us
    unnamed x1, local copies, waits for them, and re-layouts  0.97 us

profile of v2, /device:TPU:0, one launch (start us, length us, event | category | flops | bytes accessed | tf_op | source)
XLA Modules:
  0.0 21.5 jit_solution(6623981545695023044)
XLA Ops:
  0.0 20.6 %shard_map.55 = bf16[128,4096]{1,0:T(8,128)(2,1)S(1)} custom-call(bf16[128,4096]{1,0:T(8,128)(2,1)} %q_hbm.1, bf16[128,512]{1,0:T(8,128)(2,1)} %k_hbm.1, bf16[128,512]{1,0:T(8,128)(2,1)} %v_hbm.1, bf16[64,512]{1,0:T(8,128)(2,1)} %pk_hbm.1, bf16[64,512]{1,0:T(8,128)(2,1)} %pv_hbm.1), custom_call_target="tpu_custom_call" | custom-call | flops 805306368 | bytes 2097152 | tf_op jit(solution)/shard_map/pallas_call | solution.py:276
  20.6 1.0 %copy.7 = bf16[128,4096]{1,0:T(8,128)(2,1)} copy(bf16[128,4096]{1,0:T(8,128)(2,1)S(1)} %shard_map.55) | data formatting | bytes 2097152

commit v3 on v2

--- a/solution.py
+++ b/solution.py
@@ -14,20 +14,20 @@
 MESH = pl.DeviceIdType.MESH
 
 TREES = {
-    (0, 0): ((0, 2), (0, 1), (2, 4), (1, 3)),
-    (1, 0): ((1, 3), (3, 5), (3, 2), (2, 4)),
+    (0, 0): ((0, 1), (0, 2), (1, 3), (2, 4)),
+    (1, 0): ((1, 2), (1, 3), (2, 4), (3, 5)),
     (1, 1): ((1, 0),),
-    (2, 0): ((2, 4), (2, 3), (4, 6), (3, 5)),
+    (2, 0): ((2, 3), (2, 4), (3, 5), (4, 6)),
     (2, 1): ((2, 0), (0, 1)),
-    (3, 0): ((3, 5), (5, 7), (5, 4), (4, 6)),
-    (3, 1): ((3, 1), (1, 0), (0, 2)),
+    (3, 0): ((3, 5), (5, 4), (5, 6), (5, 7)),
+    (3, 1): ((3, 1), (3, 2), (1, 0)),
     (4, 0): ((4, 6), (4, 5), (6, 7)),
-    (4, 1): ((4, 2), (2, 0), (2, 3), (0, 1)),
-    (5, 0): ((5, 7), (7, 6)),
+    (4, 1): ((4, 2), (2, 0), (2, 1), (2, 3)),
+    (5, 0): ((5, 6), (5, 7)),
     (5, 1): ((5, 3), (5, 4), (3, 1), (3, 2)),
     (6, 0): ((6, 7), (7, 5)),
-    (6, 1): ((6, 4), (4, 2), (4, 5), (2, 3)),
-    (7, 0): ((7, 5), (7, 6), (5, 4)),
+    (6, 1): ((6, 4), (4, 2), (4, 3), (4, 5)),
+    (7, 0): ((7, 6), (7, 5), (6, 4)),
     (7, 1): ((7, 5), (7, 6), (5, 3), (6, 4)),
 }
 
@@ -36,6 +36,7 @@
     def __init__(self, here):
         self.here = here
         self.own, self.relays, self.leaves, self.sends, self.partners = [], [], [], [], []
+        self.deep = []
 
     def send(self, valid, source, partner, index):
         self.sends.append((valid, len(self.sends), source, partner, index))
@@ -65,7 +66,9 @@
                 index = landing(slot, half, at)
                 sends = [route.send(None, index, b, landing(slot, half, b)) for a, b in hops if a == at]
                 if slot == at:
-                    route.own.extend(sends)
+                    passing = {a for a, b in hops}
+                    for entry in sends:
+                        (route.deep if entry[3] in passing else route.own).append(entry)
                 elif at in depth and sends:
                     depths.append((depth[at], index, sends))
                 elif at in depth:
@@ -113,15 +116,6 @@
     def store_o(h):
         return pltpu.make_async_copy(o_v.at[h], o_hbm.at[:, pl.ds(h * width, width)], o_sem.at[h])
 
-    for h in range(heads):
-        for b in range(2):
-            for which in range(2):
-                load_kv(b, h, which).start()
-    for h in range(heads):
-        load_q(h).start()
-        load_pre(h, 0).start()
-        load_pre(h, 1).start()
-
     routes = programs(slots, inner, reach, me)
 
     def place(slot):
@@ -152,25 +146,36 @@
 
     def greet(route):
         barrier = pltpu.get_barrier_semaphore()
-        count = 0
         for valid, other in route.partners:
-            count = count + (1 if valid is None else valid.astype(jnp.int32))
             when(
                 valid,
                 lambda: pl.semaphore_signal(barrier, inc=1, device_id=place(other), device_id_type=MESH),
             )
-        pl.semaphore_wait(barrier, count)
 
     def each_route(body):
         for route in routes:
             when(route.here, lambda: body(route))
 
+    def all_here(route):
+        pl.semaphore_wait(pltpu.get_barrier_semaphore(), greetings(route))
+
+    def greetings(route):
+        return sum(1 if valid is None else valid.astype(jnp.int32) for valid, _ in route.partners)
+
     each_route(greet)
+    for h in range(heads):
+        for b in range(2):
+            for which in range(2):
+                load_kv(b, h, which).start()
+    each_route(all_here)
 
     def own(h):
         for b in range(2):
             for which in range(2):
                 load_kv(b, h, which).wait()
+        each_route(lambda route: start(h, route.deep))
+
+    def own_leaves(h):
         each_route(lambda route: start(h, route.own))
 
     def relay(h, level):
@@ -198,6 +203,10 @@
 
     for h in range(heads):
         own(h)
+    for h in range(heads):
+        load_q(h).start()
+        load_pre(h, 0).start()
+        load_pre(h, 1).start()
 
     rows = lax.broadcasted_iota(jnp.int32, (half, half), 0)
     cols = lax.broadcasted_iota(jnp.int32, (half, half), 1)
@@ -248,17 +257,17 @@
         def _():
             relay(h, 1)
 
-        @pl.when((h >= 1) & (h <= heads))
+        @pl.when(h < heads)
         def _():
-            relay(h - 1, 2)
-
-        @pl.when(h >= 2)
+            own_leaves(h)
+
+        @pl.when(h >= 1)
         def _():
-            head(h - 2)
+            head(h - 1)
 
         return carry
 
-    lax.fori_loop(0, heads + 2, step, 0)
+    lax.fori_loop(0, heads + 1, step, 0)
     for h in range(heads):
         drain(h)
 

time: 21.7 us -> 20.1 us (0.926)
  Pallas kernels: 20.6 us -> 19 us
    pallas_call x1, Pallas kernels: 20.6 us -> 19 us  [local(): pl.pallas_call(functools.partial(kernel, slots, inner, heads, half, reach...]
where the time goes in v3:
time: 20.1 us; the launch traced here: 20 us
  Pallas kernels  19 us (95%)
  local copies, waits for them, and re-layouts  0.97 us (5%)
    pallas_call x1, Pallas kernels, local(): pl.pallas_call(functools.partial(kernel, slots, inner, heads, half, reach...  19 us
    unnamed x1, local copies, waits for them, and re-layouts  0.97 us

profile of v3, /device:TPU:0, one launch (start us, length us, event | category | flops | bytes accessed | tf_op | source)
XLA Modules:
  0.0 20.0 jit_solution(5009111060946432508)
XLA Ops:
  0.0 19.0 %shard_map.55 = bf16[128,4096]{1,0:T(8,128)(2,1)S(1)} custom-call(bf16[128,4096]{1,0:T(8,128)(2,1)} %q_hbm.1, bf16[128,512]{1,0:T(8,128)(2,1)} %k_hbm.1, bf16[128,512]{1,0:T(8,128)(2,1)} %v_hbm.1, bf16[64,512]{1,0:T(8,128)(2,1)} %pk_hbm.1, bf16[64,512]{1,0:T(8,128)(2,1)} %pv_hbm.1), custom_call_target="tpu_custom_call" | custom-call | flops 805306368 | bytes 2097152 | tf_op jit(solution)/shard_map/pallas_call | solution.py:285
  19.0 1.0 %copy.7 = bf16[128,4096]{1,0:T(8,128)(2,1)} copy(bf16[128,4096]{1,0:T(8,128)(2,1)S(1)} %shard_map.55) | data formatting | bytes 2097152

commit v4 on v3

--- a/solution.py
+++ b/solution.py
@@ -261,13 +261,13 @@
         def _():
             own_leaves(h)
 
-        @pl.when(h >= 1)
+        @pl.when(h >= 3)
         def _():
-            head(h - 1)
+            head(h - 3)
 
         return carry
 
-    lax.fori_loop(0, heads + 1, step, 0)
+    lax.fori_loop(0, heads + 3, step, 0)
     for h in range(heads):
         drain(h)
 

time: 20.1 us -> 19.3 us (0.960)
  the two profiles are of different devices: /device:TPU:0 before, /device:TPU:20 now
where the time goes in v4:
time: 19.3 us; the launch traced here: 19.2 us
  Pallas kernels  18.2 us (94%)
  local copies, waits for them, and re-layouts  0.97 us (5%)
    pallas_call x1, Pallas kernels, local(): pl.pallas_call(functools.partial(kernel, slots, inner, heads, half, reach...  18.2 us
    unnamed x1, local copies, waits for them, and re-layouts  0.97 us

profile of v4, /device:TPU:20, one launch (start us, length us, event | category | flops | bytes accessed | tf_op | source)
XLA Modules:
  0.0 19.2 jit_solution(1876085371379284148)
XLA Ops:
  0.0 18.2 %shard_map.55 = bf16[128,4096]{1,0:T(8,128)(2,1)S(1)} custom-call(bf16[128,4096]{1,0:T(8,128)(2,1)} %q_hbm.1, bf16[128,512]{1,0:T(8,128)(2,1)} %k_hbm.1, bf16[128,512]{1,0:T(8,128)(2,1)} %v_hbm.1, bf16[64,512]{1,0:T(8,128)(2,1)} %pk_hbm.1, bf16[64,512]{1,0:T(8,128)(2,1)} %pv_hbm.1), custom_call_target="tpu_custom_call" | custom-call | flops 805306368 | bytes 2097152 | tf_op jit(solution)/shard_map/pallas_call | solution.py:285
  18.2 1.0 %copy.7 = bf16[128,4096]{1,0:T(8,128)(2,1)} copy(bf16[128,4096]{1,0:T(8,128)(2,1)S(1)} %shard_map.55) | data formatting | bytes 2097152

commit v5 on v4

--- a/solution.py
+++ b/solution.py
@@ -187,10 +187,11 @@
 
         each_route(body)
 
-    def leaves(h):
+    def leaves(h, second):
         def body(route):
             for valid, index in route.leaves:
-                arrived(h, valid, index)
+                if (index > reach) == second:
+                    arrived(h, valid, index)
 
         each_route(body)
 
@@ -236,7 +237,7 @@
         load_q(h).wait()
         load_pre(h, 0).wait()
         load_pre(h, 1).wait()
-        leaves(h)
+        leaves(h, False)
 
         zero = jnp.zeros((half, half), jnp.float32)
         blocks, biases = [0], [causal]
@@ -245,6 +246,7 @@
             blocks.append(jnp.where(there, d, 0))
             biases.append(jnp.where(there, farthest if d == reach else zero, low))
         attend(h, 0, blocks, biases)
+        leaves(h, True)
         blocks, biases = [reach + 1], [causal]
         for d in range(1, reach + 1):
             fold = 2 * slots - 1 - me - d

time: 19.3 us -> 21.3 us (1.10)
  the two profiles are of different devices: /device:TPU:20 before, /device:TPU:24 now
where the time goes in v5:
time: 21.3 us; the launch traced here: 21.1 us
  Pallas kernels  20.1 us (94%)
  local copies, waits for them, and re-layouts  0.97 us (5%)
    pallas_call x1, Pallas kernels, local(): pl.pallas_call(functools.partial(kernel, slots, inner, heads, half, reach...  20.1 us
    unnamed x1, local copies, waits for them, and re-layouts  0.97 us

profile of v5, /device:TPU:24, one launch (start us, length us, event | category | flops | bytes accessed | tf_op | source)
XLA Modules:
  0.0 21.1 jit_solution(6655785248890188013)
XLA Ops:
  0.0 20.1 %shard_map.55 = bf16[128,4096]{1,0:T(8,128)(2,1)S(1)} custom-call(bf16[128,4096]{1,0:T(8,128)(2,1)} %q_hbm.1, bf16[128,512]{1,0:T(8,128)(2,1)} %k_hbm.1, bf16[128,512]{1,0:T(8,128)(2,1)} %v_hbm.1, bf16[64,512]{1,0:T(8,128)(2,1)} %pk_hbm.1, bf16[64,512]{1,0:T(8,128)(2,1)} %pv_hbm.1), custom_call_target="tpu_custom_call" | custom-call | flops 805306368 | bytes 2097152 | tf_op jit(solution)/shard_map/pallas_call | solution.py:287
  20.2 1.0 %copy.7 = bf16[128,4096]{1,0:T(8,128)(2,1)} copy(bf16[128,4096]{1,0:T(8,128)(2,1)S(1)} %shard_map.55) | data formatting | bytes 2097152
